TPU v7x, 256 devices: a whole 4x4x8 slice. The times are simulated.
256 devices in a mesh: prow: 8 (over x, y_lo), pcol: 32 (over y_hi, z, core).
Axes of the slice: x: 4, y: 4 (y_hi: 2, y_lo: 2; y = y_hi * 2 + y_lo), z: 8, core: 2. Of those that a mesh axis runs over, the one named last changes fastest.
Arguments:
- anc_inverse: bfloat16 [12, 2048, 3, 8192], P(None, 'prow', None, 'pcol'), may hold values from -0.0390625 to 0.0390625
- panel: bfloat16 [3, 12, 8, 256, 512], P(None, None, 'prow', 'pcol'), may hold values from -1.1953125 to 1.1953125
- tile_mask: int32 [3, 96], replicated, may hold values 0 or 1
- diag_inverse: float32 [3, 512, 512], P(None, ('prow', 'pcol')), may hold values from -6 to 6
Outputs:
- block_column: bfloat16 [3, 12, 8, 256, 512], P(None, None, 'prow', 'pcol')
- diag_block: float32 [3, 512, 512], P(None, ('prow', 'pcol'))
All inputs are finite; a program needn't handle non-finite values.
Results may differ from a plain program's by a relative error of at most 0.0017.
Values may be sent and summed in bfloat16 or wider, within the bound.
A program may use at most 128 MiB of HBM per device.

v0:
```python
import jax
import jax.numpy as jnp
from jax import lax
from jax.sharding import PartitionSpec as P


def spread(x, axis, root):
    mine = lax.axis_index(axis) == root
    return lax.psum(jnp.where(mine, x, jnp.zeros_like(x)), axis)


def local_product(anc_block, columns):
    return jnp.einsum("aibj,sbjw->isaw", anc_block, columns, preferred_element_type=jnp.float32)


def outbound(masked, n_row, n_col):
    groups, tile_rows, single, sub_rows, width = masked.shape
    tile_cols = tile_rows * n_row // n_col
    grouped = masked.reshape(groups, tile_cols, n_col // n_row, sub_rows, width)
    return jnp.repeat(grouped, n_row, axis=2)


def body(anc_inverse, panel, tile_mask, diag_inverse):
    n_row = lax.axis_size("prow")
    n_col = lax.axis_size("pcol")
    row_pos = lax.axis_index("prow")
    col_pos = lax.axis_index("pcol")
    sets, tile_rows, single, sub_rows, width = panel.shape
    tiles = tile_mask.shape[1]
    tile_size = anc_inverse.shape[1]
    row_ids = jnp.arange(tile_rows, dtype=jnp.int32) * n_row + row_pos
    hits = (row_ids[:, None] == jnp.arange(tiles, dtype=jnp.int32)[None, :]).astype(jnp.int32)
    row_mask = jnp.sum(tile_mask[:, None, :] * hits[None], axis=2)
    keep = row_mask.astype(jnp.bfloat16)[:, :, None, None, None]
    masked = panel * keep
    outgoing = outbound(masked, n_row, n_col)
    root = col_pos % n_row
    pieces = []
    for index in range(sets):
        arrived = lax.all_to_all(
            outgoing[index : index + 1], "pcol", split_axis=2, concat_axis=3, tiled=True
        )
        columns = spread(arrived.reshape(1, -1, tile_size, width), "prow", root)
        pieces.append(
            lax.psum_scatter(
                local_product(anc_inverse, columns), "pcol", scatter_dimension=0, tiled=True
            )
        )
    summed = jnp.concatenate(pieces, axis=1)
    image = -jnp.transpose(summed, (1, 2, 0, 3))[:, :, None] * keep.astype(jnp.float32)
    block_column = image.astype(jnp.bfloat16)
    partial_value = jnp.einsum(
        "saxiw,saxiv->swv", masked, block_column, preferred_element_type=jnp.float32
    )
    mine = lax.psum_scatter(partial_value, ("prow", "pcol"), scatter_dimension=1, tiled=True)
    diag_block = diag_inverse - mine
    return (block_column, diag_block)


def solution(mesh):
    in_specs = (
        P(None, "prow", None, "pcol"),
        P(None, None, "prow", "pcol", None),
        P(),
        P(None, ("prow", "pcol"), None),
    )
    out_specs = (P(None, None, "prow", "pcol", None), P(None, ("prow", "pcol"), None))
    return jax.shard_map(body, mesh=mesh, in_specs=in_specs, out_specs=out_specs, check_vma=False)
```

profile of v0, /device:TPU:24, one launch (start us, length us, event | category | flops | bytes accessed | tf_op | source)
XLA Modules:
  0.0 1113.9 jit_solution(5080620004551118241)
XLA Ops:
  7.2 0.1 fusion.10
  7.3 0.8 multiply_reduce_fusion
  8.1 1.1 broadcast_multiply_fusion
  9.2 1.0 broadcast_in_dim.23
  10.2 11.6 %all-to-all-start.2 = ((bf16[1,3,32,8,512]{4,3,1,0,2:T(8,128)(2,1)}), bf16[1,3,32,8,512]{4,3,1,0,2:T(8,128)(2,1)S(1)}, u32[]{:S(2)}, u32[]{:S(2)}) async-start(bf16[1,3,32,8,512]{4,3,1,0,2:T(8,128)(2,1)} %bitcast.17), calls=%async_computation.2 | async-start | bytes 1572864 | tf_op jit(solution)/shard_map/all_to_all | solution.py:40
  21.8 22.4 %all-to-all-done.2 = bf16[1,3,32,8,512]{4,3,1,0,2:T(8,128)(2,1)S(1)} async-done(((bf16[1,3,32,8,512]{4,3,1,0,2:T(8,128)(2,1)}), bf16[1,3,32,8,512]{4,3,1,0,2:T(8,128)(2,1)S(1)}, u32[]{:S(2)}, u32[]{:S(2)}) %all-to-all-start.2) | async-done | bytes 786464 | tf_op jit(solution)/shard_map/all_to_all | solution.py:40
  44.2 1.0 broadcast_in_dim.21
  45.1 6.3 all-to-all-start.1
  51.5 22.3 %all-to-all-done.1 = bf16[1,3,32,8,512]{4,3,1,0,2:T(8,128)(2,1)S(1)} async-done(((bf16[1,3,32,8,512]{4,3,1,0,2:T(8,128)(2,1)}), bf16[1,3,32,8,512]{4,3,1,0,2:T(8,128)(2,1)S(1)}, u32[]{:S(2)}, u32[]{:S(2)}) %all-to-all-start.1) | async-done | bytes 786464 | tf_op jit(solution)/shard_map/all_to_all | solution.py:40
  73.8 1.0 broadcast_in_dim.19
  74.7 6.4 all-to-all-start
  81.2 0.0 all-reduce.17.cloned.1.call-start
  81.2 0.1 fusion.3
  81.3 1.2 copy.44
  82.5 0.1 fusion.4
  82.6 1.2 copy.40
  83.7 19.8 %all-to-all-done = bf16[1,3,32,8,512]{4,3,1,0,2:T(8,128)(2,1)S(1)} async-done(((bf16[1,3,32,8,512]{4,3,1,0,2:T(8,128)(2,1)}), bf16[1,3,32,8,512]{4,3,1,0,2:T(8,128)(2,1)S(1)}, u32[]{:S(2)}, u32[]{:S(2)}) %all-to-all-start) | async-done | bytes 786464 | tf_op jit(solution)/shard_map/all_to_all | solution.py:40
  103.5 0.1 fusion.5
  103.5 1.2 copy.36
  104.7 0.0 all-reduce.17.cloned.1.call-update
  104.7 0.0 all-reduce.11.cloned.1.call-start
  104.8 117.0 %all-reduce.17.cloned.1.call-done = (bf16[3,256,512]{1,2,0:T(8,128)(2,1)}, bf16[3,256,512]{1,2,0:T(8,128)(2,1)}, bf16[3,256,512]{1,2,0:T(8,128)(2,1)}) async-done(((bf16[3,256,512]{1,2,0:T(8,128)(2,1)}, bf16[3,256,512]{1,2,0:T(8,128)(2,1)}, bf16[3,256,512]{1,2,0:T(8,128)(2,1)}), (bf16[3,256,512]{1,2,0:T(8,128)(2,1)}, bf16[3,256,512]{1,2,0:T(8,128)(2,1)}, ...) | async-done | bytes 2359312 | tf_op jit(solution)/shard_map/psum | solution.py:9
  221.8 7.9 convolution_bitcast_fusion.2
  229.7 16.0 %copy.37 = f32[256,1,12,512]{3,1,2,0:T(1,128)} copy(f32[256,1,12,512]{0,3,2,1:T(8,128)} %convolution_bitcast_fusion.2) | data formatting | bytes 12582912 | tf_op jit(solution)/shard_map/aibj,sbjw->isaw/transpose | solution.py:13
  245.7 0.0 all-reduce.11.cloned.1.call-update
  245.7 0.0 all-reduce.15.cloned.1.call-start
  245.8 1.1 copy-done.2
  246.8 6.9 convolution_bitcast_fusion
  253.7 16.1 %copy.45 = f32[256,1,12,512]{3,1,2,0:T(1,128)} copy(f32[256,1,12,512]{0,3,2,1:T(8,128)} %convolution_bitcast_fusion) | data formatting | bytes 12582912 | tf_op jit(solution)/shard_map/aibj,sbjw->isaw/transpose | solution.py:13
  269.7 6.9 convolution_bitcast_fusion.1
  276.6 16.1 %copy.41 = f32[256,1,12,512]{3,1,2,0:T(1,128)} copy(f32[256,1,12,512]{0,3,2,1:T(8,128)} %convolution_bitcast_fusion.1) | data formatting | bytes 12582912 | tf_op jit(solution)/shard_map/aibj,sbjw->isaw/transpose | solution.py:13
  292.7 0.0 all-reduce.15.cloned.1.call-update
  292.7 0.0 all-reduce.13.cloned.1.call-start
  292.8 0.6 copy-done.3
  293.4 0.6 dynamic-slice
  294.6 236.7 %all-reduce.11.cloned.1.call-done = f32[256,1,12,512]{3,1,2,0:T(1,128)} async-done(((f32[256,1,12,512]{3,1,2,0:T(1,128)}), f32[256,1,12,512]{3,1,2,0:T(1,128)}) %all-reduce.11.cloned.1.call-update) | async-done | bytes 6291472
  531.3 0.9 constant_dynamic-slice_fusion.2
  532.3 0.1 copy.46
  532.4 304.1 %all-reduce.15.cloned.1.call-done = (f32[256,1,12,512]{3,1,2,0:T(1,128)}, f32[256,1,12,512]{3,1,2,0:T(1,128)}) async-done(((f32[256,1,12,512]{3,1,2,0:T(1,128)}, f32[256,1,12,512]{3,1,2,0:T(1,128)}), (f32[256,1,12,512]{3,1,2,0:T(1,128)}, f32[256,1,12,512]{3,1,2,0:T(1,128)})) %all-reduce.15.cloned.1.call-update) | async-done | bytes 12582928
  836.5 1.3 constant_dynamic-slice_fusion
  837.8 0.1 copy.48
  837.9 0.1 copy.47
  838.0 0.0 copy-start
  838.0 2.3 convolution_bitcast_fusion.3
  840.3 0.0 all-reduce.13.cloned.1.call-update
  840.3 0.8 fusion.11
  841.1 264.8 %all-reduce.13.cloned.1.call-done = f32[3,512,512]{2,1,0:T(8,128)} async-done(((f32[3,512,512]{2,1,0:T(8,128)}), f32[3,512,512]{2,1,0:T(8,128)}) %all-reduce.13.cloned.1.call-update) | async-done | bytes 3145744
  1106.0 1.4 dynamic-slice_subtract_fusion
  (11 shorter events, 0.1 us)
Async XLA Ops:
  10.2 34.0 %all-to-all-start.2 = ((bf16[1,3,32,8,512]{4,3,1,0,2:T(8,128)(2,1)}), bf16[1,3,32,8,512]{4,3,1,0,2:T(8,128)(2,1)S(1)}, u32[]{:S(2)}, u32[]{:S(2)}) async-start(bf16[1,3,32,8,512]{4,3,1,0,2:T(8,128)(2,1)} %bitcast.17), calls=%async_computation.2 | async-start | bytes 1572864 | tf_op jit(solution)/shard_map/all_to_all | solution.py:40
  45.1 28.7 %all-to-all-start.1 = ((bf16[1,3,32,8,512]{4,3,1,0,2:T(8,128)(2,1)}), bf16[1,3,32,8,512]{4,3,1,0,2:T(8,128)(2,1)S(1)}, u32[]{:S(2)}, u32[]{:S(2)}) async-start(bf16[1,3,32,8,512]{4,3,1,0,2:T(8,128)(2,1)} %bitcast.9), calls=%async_computation.1 | async-start | bytes 1572864 | tf_op jit(solution)/shard_map/all_to_all | solution.py:40
  74.7 28.7 %all-to-all-start = ((bf16[1,3,32,8,512]{4,3,1,0,2:T(8,128)(2,1)}), bf16[1,3,32,8,512]{4,3,1,0,2:T(8,128)(2,1)S(1)}, u32[]{:S(2)}, u32[]{:S(2)}) async-start(bf16[1,3,32,8,512]{4,3,1,0,2:T(8,128)(2,1)} %bitcast.1), calls=%async_computation | async-start | bytes 1572864 | tf_op jit(solution)/shard_map/all_to_all | solution.py:40
  81.2 140.6 %all-reduce.17.cloned.1.call-start = ((), (), s32[]{:S(2)}) async-start(), calls=%async_computation.6 | async-start | bytes 4718592 | tf_op jit(solution)/shard_map/psum | solution.py:9
  104.7 426.6 %all-reduce.11.cloned.1.call-start = ((), (), s32[]{:S(2)}) async-start(), calls=%async_computation.3 | async-start | bytes 12582912
  245.7 1.1 copy-start.2
  245.7 590.8 %all-reduce.15.cloned.1.call-start = ((), (), s32[]{:S(2)}) async-start(), calls=%async_computation.5 | async-start | bytes 25165824
  253.7 16.1 %copy-start.1 = (bf16[3,256,512]{1,2,0:T(8,128)(2,1)S(1)}, bf16[3,256,512]{1,2,0:T(8,128)(2,1)}, u32[]{:S(2)}) copy-start(bf16[3,256,512]{1,2,0:T(8,128)(2,1)} %get-tuple-element.13) | copy-start | bytes 2359300
  292.7 0.7 copy-start.3
  292.7 813.2 %all-reduce.13.cloned.1.call-start = ((), (), s32[]{:S(2)}) async-start(), calls=%async_computation.4 | async-start | bytes 6291456
  838.0 268.0 %copy-start = (f32[3,2,512]{2,1,0:T(2,128)S(1)}, f32[3,2,512]{2,1,0:T(2,128)}, u32[]{:S(2)}) copy-start(f32[3,2,512]{2,1,0:T(2,128)} %param.7) | copy-start | bytes 36868
Sparse Core Ops, SparseCore 0:
  104.8 116.8 all-reduce.16
  245.8 285.4 all-reduce.10
  534.1 302.3 all-reduce.14
  841.8 264.1 all-reduce.12
where the time goes:
time: 1120 us; the launch traced here: 1110 us
  waiting for transfers between devices  987 us (88%)
  local copies, waits for them, and re-layouts  59.3 us (5%)
  starting transfers between devices  24.5 us (2%)
  matrix products  23.9 us (2%)
  between operations  14.6 us (1%)
    unnamed x7, waiting for transfers between devices  806 us
    psum x1, waiting for transfers between devices, spread(): return lax.psum(jnp.where(mine, x, jnp.zeros_like(x)), axis)  117 us
    all_to_all x3, waiting for transfers between devices, body(): lax.all_to_all(outgoing[index:index + 1], 'pcol', split_axis=2, concat_ax...  64.4 us
    transpose x3, local copies, waits for them, and re-layouts, local_product(): jnp.einsum('aibj,sbjw->isaw', anc_block, columns, preferred_element_type=...  48.2 us
    all_to_all x3, starting transfers between devices, body(): lax.all_to_all(outgoing[index:index + 1], 'pcol', split_axis=2, concat_ax...  24.4 us
  transfers between devices with their start and end apart: 7, of which 7 were waited for; matrix products, arithmetic and copies ran while one was open for 5% of the time, Pallas kernels for 0%

commit v1 on v0

v1 whole, which is shorter than its diff:
```python
import functools

import jax
import jax.numpy as jnp
from jax import lax
from jax.experimental import pallas as pl
from jax.experimental.pallas import tpu as pltpu
from jax.sharding import PartitionSpec as P

MESH = pl.DeviceIdType.MESH
F32 = jnp.float32
BF16 = jnp.bfloat16
I16 = jnp.int16
SUB = 8
LEVELS = 32000.0
LAG = 2


def kernel(
    NP, NCOL, mask_ref, anc_ref, panel_ref, dinv_ref, col_ref, diag_ref,
    mfull, mf, sib, mpair, lbuf, cbuf, sbuf, rbuf, ysb, yrb, colp, perm, mpt,
    dsend, drecv, esend, erecv,
    m_l, m_s, m_r, a0_s, a0_r, a1_s, a1_r, a2_s, a2_r, a3_s, a3_r,
    r_s, r_r, y_s, y_r, c_s, c_r, d_s, d_r, e_s, e_r,
):
    SETS, RT, _, W = panel_ref.shape
    CT = anc_ref.shape[1]
    TILE = anc_ref.shape[2]
    HALF = RT // 2
    NC = NCOL // 2
    Z = NC // 2
    NH = NCOL // NP
    NT = 2 * NP
    LC = W // 4
    WH = W // 2
    TH = HALF // 2
    ROWS = HALF * 16
    NG = ROWS // SUB
    HOPS = Z - 1

    p = lax.axis_index("prow")
    q = lax.axis_index("pcol")
    core = lax.rem(q, 2)
    chip = q // 2
    z = lax.rem(chip, Z)
    yh = chip // Z
    sibling = (p, q + 1 - 2 * core)
    t_me = p * 2 + yh

    def at_chip(row, y, depth):
        return (row, (y * Z + depth) * 2 + core)

    def plane(step):
        other = lax.rem(t_me + step, NT)
        return at_chip(other // 2, lax.rem(other, 2), z)

    up = at_chip(p, yh, lax.rem(z + 1, Z))
    down = at_chip(p, yh, lax.rem(z + Z - 1, Z))
    y_mate = at_chip(p, 1 - yh, z)

    a1_row = lax.rem(chip, NP)
    a1_core = chip // NP

    def a1_target(h2):
        h = 2 * core + h2
        return (a1_row, 2 * (h * (NP // 2) + p // 2) + a1_core)

    def a1_is_me(h2):
        row, column = a1_target(h2)
        return jnp.logical_and(row == p, column == q)

    def a1_source(half):
        return (2 * lax.rem(chip, NP // 2) + half, 2 * (core * NP + p) + yh)

    def signal(where):
        pl.semaphore_signal(barrier, inc=1, device_id=where, device_id_type=MESH)

    barrier = pltpu.get_barrier_semaphore()
    signal(sibling)

    @pl.loop(1, NT)
    def _(step):
        signal(plane(step))

    @pl.loop(1, Z)
    def _(step):
        signal(at_chip(p, yh, lax.rem(z + step, Z)))

    expected = 1 + (NT - 1) + (Z - 1)
    for e in range(2):
        me = a1_is_me(e)
        row, column = a1_source(e)
        from_me = jnp.logical_and(row == p, column == q)

        @pl.when(jnp.logical_not(me))
        def _():
            signal(a1_target(e))

        @pl.when(jnp.logical_not(from_me))
        def _():
            signal((row, column))

        expected = expected + jnp.where(me, 0, 1) + jnp.where(from_me, 0, 1)

    def copy(src, dst, send, recv, where):
        return pltpu.make_async_remote_copy(
            src_ref=src, dst_ref=dst, send_sem=send, recv_sem=recv,
            device_id=where, device_id_type=MESH,
        )

    def lanes(half, b):
        return pl.ds(pl.multiple_of((half * CT + b) * TILE, TILE), TILE)

    def m_local(b):
        return pltpu.make_async_copy(
            anc_ref.at[pl.ds(core * HALF, HALF), b], mfull.at[:, :, lanes(core, b)], m_l.at[b])

    def m_swap(b):
        return copy(
            anc_ref.at[pl.ds((1 - core) * HALF, HALF), b], mfull.at[:, :, lanes(core, b)],
            m_s.at[b], m_r.at[b], sibling)

    for b in range(CT):
        m_local(b).start()

    def keep(s, a):
        return mask_ref[s, a * NP + p].astype(F32)

    @pl.loop(0, SETS)
    def _(s):
        @pl.loop(0, RT)
        def _(a):
            mf[s, a] = panel_ref[s, a].astype(F32) * keep(s, a)

    rows = lax.broadcasted_iota(jnp.int32, (WH, W), 0)
    columns = lax.broadcasted_iota(jnp.int32, (WH, W), 1)
    hit = columns == (rows >> 1) * 4 + 2 * core + (rows & 1)
    perm[...] = jnp.where(hit, 1.0, 0.0).astype(BF16)

    pl.semaphore_wait(barrier, expected)

    def a0(s):
        return copy(mf.at[s], sib.at[s], a0_s.at[s], a0_r.at[s], sibling)

    for s in range(SETS):
        a0(s).start()
    for b in range(CT):
        m_swap(b).start()

    def l_slice(s, index):
        return lbuf.at[s, :, pl.ds(pl.multiple_of(16 * index, 16), 16), :]

    def a1_dst(s):
        return lbuf.at[s, pl.ds(lax.rem(p, 2) * CT, CT), pl.ds(pl.multiple_of(16 * chip, 16), 16), :]

    def a1(s, h2):
        return copy(mpair.at[s, :, 2 * core + h2], a1_dst(s), a1_s.at[s, h2], a1_r.at[s], a1_target(h2))

    def a1_local(s, h2):
        return pltpu.make_async_copy(mpair.at[s, :, 2 * core + h2], a1_dst(s), a1_r.at[s])

    mine = core * NP + p

    def a1_wait(s):
        copy(l_slice(s, mine), l_slice(s, mine), a1_s.at[s, 0], a1_r.at[s], sibling).wait_recv()

    @pl.loop(0, SETS)
    def _(s):
        a0(s).wait_recv()
        own = mf[s]
        other = sib[s]
        low = jnp.where(core == 0, own, other)
        high = jnp.where(core == 0, other, own)
        both = jnp.concatenate([low, high], axis=1)
        mpair[s] = both.astype(BF16).reshape(CT, NH, 16, W)
        for h2 in range(2):
            me = a1_is_me(h2)

            @pl.when(me)
            def _():
                a1_local(s, h2).start()

            @pl.when(jnp.logical_not(me))
            def _():
                a1(s, h2).start()

        mpt[s] = lax.dot_general(
            perm[...], mpair[s].reshape(RT * 16, W), (((1,), (1,)), ((), ())),
            preferred_element_type=F32).astype(BF16)

    def a2(s, step):
        where = (lax.rem(p + step, NP), q)
        return copy(l_slice(s, mine), l_slice(s, mine), a2_s.at[s, step], a2_r.at[s, step], where)

    def a2_sibling(s):
        return copy(l_slice(s, mine), l_slice(s, mine), a2_s.at[s, 0], a2_r.at[s, 0], sibling)

    def a3(s, step):
        index = core * NP + lax.rem(p + NP - step, NP)
        return copy(l_slice(s, index), l_slice(s, index), a3_s.at[s, step], a3_r.at[s, step], sibling)

    def spread(s):
        a1_wait(s)

        @pl.loop(1, NP)
        def _(step):
            a2(s, step).start()

        a2_sibling(s).start()

    def piece(s, d, depth, j):
        return (s, pl.ds(d * TH, TH), slice(None), depth, slice(None), pl.ds(j * LC, LC))

    def y_piece(s, y, j):
        return (s, slice(None), y, z, slice(None), pl.ds(j * LC, LC))

    def pack(index, dst):
        top = jnp.zeros((SUB, LC), F32)
        for j in range(4):
            v = cbuf[index(j)].reshape(NG, SUB, LC)
            top = jnp.maximum(top, jnp.max(jnp.abs(v), axis=0))
        power = jnp.minimum(jnp.maximum(jnp.ceil(jnp.log2(top)), -100.0), 100.0)
        factor = jnp.exp2(-power) * LEVELS
        for j in range(4):
            v = cbuf[index(j)].reshape(NG, SUB, LC) * factor[None]
            whole = jnp.round(v).astype(jnp.int32).astype(I16)
            dst[pl.ds(j * ROWS, ROWS), :] = whole.reshape(ROWS, LC)
        power = power.astype(jnp.int32)
        dst[pl.ds(4 * ROWS, 16), :] = jnp.concatenate([power, power], axis=0).astype(I16)

    def scale_of(src):
        power = src[pl.ds(4 * ROWS, 16), :].astype(jnp.int32).astype(F32)[:SUB]
        return jnp.exp2(power) * (1.0 / LEVELS)

    def unpack(src, scale, j):
        v = src[pl.ds(j * ROWS, ROWS), :].astype(jnp.int32).astype(F32)
        return v.reshape(NG, SUB, LC) * scale[None]

    def hop_chunk(d, k):
        return lax.rem(jnp.where(d == 0, z + 2 * Z - 1 - k, z + 1 + k), Z)

    def hop(s, d, k):
        where = (p, jnp.where(d == 0, up[1], down[1]))
        return copy(sbuf.at[s, d, k], rbuf.at[s, d, k], r_s.at[s, d, k], r_r.at[s, d, k], where)

    def ring_step(s, d, k):
        depth = hop_chunk(d, k)

        @pl.when(k > 0)
        def _():
            hop(s, d, k - 1).wait_recv()
            src = rbuf.at[s, d, k - 1]
            scale = scale_of(src)
            for j in range(4):
                index = piece(s, d, depth, j)
                shape = (TH, 2, 16, LC)
                cbuf[index] = cbuf[index] + unpack(src, scale, j).reshape(shape)

        @pl.when(k < HOPS)
        def _():
            pack(lambda j: piece(s, d, depth, j), sbuf.at[s, d, k])
            hop(s, d, k).start()

    def y_copy(s):
        return copy(ysb.at[s], yrb.at[s], y_s.at[s], y_r.at[s], y_mate)

    def c_copy(s):
        return copy(colp.at[s, core], colp.at[s, core], c_s.at[s], c_r.at[s], sibling)

    def arrive(s):
        @pl.loop(1, NP)
        def _(step):
            a2(s, step).wait_recv()
            a3(s, step).start()

        @pl.when(s + 1 < SETS)
        def _():
            spread(s + 1)

        a2_sibling(s).wait_recv()

        @pl.loop(1, NP)
        def _(step):
            a3(s, step).wait_recv()

        @pl.when(s == 0)
        def _():
            for b in range(CT):
                m_local(b).wait()
                m_swap(b).wait_recv()

        @pl.loop(0, HALF)
        def _(a):
            product = jnp.dot(
                mfull[a], lbuf[s].reshape(2 * CT * TILE, W), preferred_element_type=F32)
            cbuf[s, a] = product.reshape(2, Z, 16, W)

    def y_arrive(s):
        y_copy(s).wait_recv()
        src = yrb.at[s]
        scale = scale_of(src)
        for j in range(4):
            total = cbuf[y_piece(s, yh, j)] + unpack(src, scale, j).reshape(HALF, 16, LC)
            for a in range(HALF):
                image = -total[a] * keep(s, core * HALF + a)
                colp[s, core, a, :, pl.ds(j * LC, LC)] = image.astype(BF16)
        c_copy(s).start()

    def d_copy(s, step):
        other = lax.rem(t_me + step, NT)
        return copy(dsend.at[s, other], drecv.at[s, step], d_s.at[s, step], d_r.at[s, step], plane(step))

    def c_arrive(s):
        c_copy(s).wait_recv()
        dsend[s] = jnp.dot(
            mpt[s], colp[s].reshape(RT * 16, W), preferred_element_type=F32).reshape(NT, 2 * Z, W)

        @pl.loop(1, NT)
        def _(step):
            d_copy(s, step).start()

        both = colp[s].reshape(RT, 16, W).astype(F32)
        picked = jnp.where(core == 0, both[:, :SUB], both[:, SUB:])
        col_ref[s] = picked.astype(BF16)

    def d_arrive(s):
        @pl.loop(1, NT)
        def _(step):
            d_copy(s, step).wait_recv()

        total = dsend[s, t_me]
        for step in range(1, NT):
            total = total + drecv[s, step]
        for depth in range(Z):
            esend[depth, s] = total[2 * depth : 2 * depth + 2]

    spread(0)

    @pl.loop(0, (SETS - 1) * LAG + HOPS + 4)
    def _(t):
        @pl.loop(0, SETS)
        def _(s):
            k = t - s * LAG

            @pl.when(k == 0)
            def _():
                arrive(s)

            @pl.when(jnp.logical_and(k >= 0, k <= HOPS))
            def _():
                @pl.loop(0, 2)
                def _(d):
                    ring_step(s, d, k)

            @pl.when(k == HOPS)
            def _():
                pack(lambda j: y_piece(s, 1 - yh, j), ysb.at[s])
                y_copy(s).start()

            @pl.when(k == HOPS + 1)
            def _():
                y_arrive(s)

            @pl.when(k == HOPS + 2)
            def _():
                c_arrive(s)

            @pl.when(k == HOPS + 3)
            def _():
                d_arrive(s)

    def e_copy(step):
        other = lax.rem(z + step, Z)
        return copy(esend.at[other], erecv.at[step], e_s.at[step], e_r.at[step], at_chip(p, yh, other))

    @pl.loop(1, Z)
    def _(step):
        e_copy(step).start()

    @pl.loop(1, Z)
    def _(step):
        e_copy(step).wait_recv()

    total = esend[z]
    for step in range(1, Z):
        total = total + erecv[step]
    diag_ref[...] = dinv_ref[...] - total

    for b in range(CT):
        m_swap(b).wait_send()

    @pl.loop(0, SETS)
    def _(s):
        a0(s).wait_send()
        for h2 in range(2):
            @pl.when(jnp.logical_not(a1_is_me(h2)))
            def _():
                a1(s, h2).wait_send()

        a2_sibling(s).wait_send()

        @pl.loop(1, NP)
        def _(step):
            a2(s, step).wait_send()
            a3(s, step).wait_send()

        @pl.loop(0, HOPS)
        def _(k):
            hop(s, 0, k).wait_send()
            hop(s, 1, k).wait_send()

        y_copy(s).wait_send()
        c_copy(s).wait_send()

        @pl.loop(1, NT)
        def _(step):
            d_copy(s, step).wait_send()

    @pl.loop(1, Z)
    def _(step):
        e_copy(step).wait_send()


def body(anc_inverse, panel, tile_mask, diag_inverse):
    n_row = lax.axis_size("prow")
    n_col = lax.axis_size("pcol")
    sets, rt, _, sub, w = panel.shape
    _, tile, ct, _ = anc_inverse.shape
    anc = jnp.transpose(anc_inverse, (0, 2, 1, 3))
    slim = panel.reshape(sets, rt, sub, w)
    half, nz, nt, nh = rt // 2, n_col // 4, 2 * n_row, n_col // n_row
    hops = nz - 1
    lc = w // 4
    message = 4 * half * 16 + 16
    dma = pltpu.SemaphoreType.DMA
    vmem = pl.BlockSpec(memory_space=pltpu.VMEM)
    scratch = [
        pltpu.VMEM((half, tile, 2 * ct * tile), BF16),
        pltpu.VMEM((sets, rt, sub, w), F32),
        pltpu.VMEM((sets, rt, sub, w), F32),
        pltpu.VMEM((sets, ct, nh, 16, w), BF16),
        pltpu.VMEM((sets, 2 * ct, tile, w), BF16),
        pltpu.VMEM((sets, half, 2, nz, 16, w), F32),
        pltpu.VMEM((sets, 2, hops, message, lc), I16),
        pltpu.VMEM((sets, 2, hops, message, lc), I16),
        pltpu.VMEM((sets, message, lc), I16),
        pltpu.VMEM((sets, message, lc), I16),
        pltpu.VMEM((sets, 2, half, 16, w), BF16),
        pltpu.VMEM((w // 2, w), BF16),
        pltpu.VMEM((sets, w // 2, rt * 16), BF16),
        pltpu.VMEM((sets, nt, 2 * nz, w), F32),
        pltpu.VMEM((sets, nt, 2 * nz, w), F32),
        pltpu.VMEM((nz, sets, 2, w), F32),
        pltpu.VMEM((nz, sets, 2, w), F32),
        dma((ct,)), dma((ct,)), dma((ct,)),
        dma((sets,)), dma((sets,)),
        dma((sets, 2)), dma((sets,)),
        dma((sets, n_row)), dma((sets, n_row)),
        dma((sets, n_row)), dma((sets, n_row)),
        dma((sets, 2, hops)), dma((sets, 2, hops)),
        dma((sets,)), dma((sets,)),
        dma((sets,)), dma((sets,)),
        dma((sets, nt)), dma((sets, nt)),
        dma((nz,)), dma((nz,)),
    ]
    column, diag = pl.pallas_call(
        functools.partial(kernel, n_row, n_col),
        out_shape=(
            jax.ShapeDtypeStruct((sets, rt, sub, w), BF16),
            jax.ShapeDtypeStruct(diag_inverse.shape, F32),
        ),
        in_specs=[
            pl.BlockSpec(memory_space=pltpu.SMEM),
            pl.BlockSpec(memory_space=pl.ANY),
            vmem,
            vmem,
        ],
        out_specs=(vmem, vmem),
        scratch_shapes=scratch,
        compiler_params=pltpu.CompilerParams(
            collective_id=0, has_side_effects=True, vmem_limit_bytes=56 * 1024 * 1024
        ),
        name="selected_inverse",
    )(tile_mask, anc, slim, diag_inverse)
    return column.reshape(panel.shape), diag


def solution(mesh):
    in_specs = (
        P(None, "prow", None, "pcol"),
        P(None, None, "prow", "pcol", None),
        P(),
        P(None, ("prow", "pcol"), None),
    )
    out_specs = (P(None, None, "prow", "pcol", None), P(None, ("prow", "pcol"), None))
    return jax.shard_map(body, mesh=mesh, in_specs=in_specs, out_specs=out_specs, check_vma=False)
```

time: 1120 us -> 143 us (0.13)
  waiting for transfers between devices: 987 us -> 0 us
  Pallas kernels: 0 us -> 140 us
  local copies, waits for them, and re-layouts: 59.3 us -> 3 us
  starting transfers between devices: 24.5 us -> 0 us
  matrix products: 23.9 us -> 0 us
  between operations: 14.6 us -> 0.64 us
    unnamed x7 -> x0, waiting for transfers between devices: 806 us -> none
    pallas_call x0 -> x1, Pallas kernels: none -> 140 us  [body(): pl.pallas_call(functools.partial(kernel, n_row, n_col), out_shape=(jax.Sh...]
    psum x1 -> x0, waiting for transfers between devices: 117 us -> none  [spread(): return lax.psum(jnp.where(mine, x, jnp.zeros_like(x)), axis)]
    all_to_all x3 -> x0, waiting for transfers between devices: 64.4 us -> none  [body(): lax.all_to_all(outgoing[index:index + 1], 'pcol', split_axis=2, concat_ax...]
    transpose x3 -> x0, local copies, waits for them, and re-layouts: 48.2 us -> none  [local_product(): jnp.einsum('aibj,sbjw->isaw', anc_block, columns, preferred_element_type=...]
    all_to_all x3 -> x0, starting transfers between devices: 24.4 us -> none  [body(): lax.all_to_all(outgoing[index:index + 1], 'pcol', split_axis=2, concat_ax...]
    dot_general x4 -> x0, matrix products: 23.9 us -> none  [the longest x3 21.6 us: local_product(): jnp.einsum('aibj,sbjw->isaw', anc_block, columns, preferred_element_type=...]
  transfers between devices with their start and end apart: 7 -> 0, of which waited for: 7 -> 0; matrix products, arithmetic and copies ran while one was open for 5% -> 0% of each run, Pallas kernels for 0% -> 0%
where the time goes in v1:
time: 143 us
  Pallas kernels  140 us (98%)
  local copies, waits for them, and re-layouts  3 us (2%)
    pallas_call x1, Pallas kernels, body(): pl.pallas_call(functools.partial(kernel, n_row, n_col), out_shape=(jax.Sh...  140 us
    unnamed x2, local copies, waits for them, and re-layouts  3 us

profile of v1, /device:TPU:24, one launch (start us, length us, event | category | flops | bytes accessed | tf_op | source)
XLA Modules:
  0.0 143.2 jit_solution(2466266584608457997)
XLA Ops:
  0.6 139.5 %selected_inverse.1 = (bf16[3,12,8,512]{3,2,1,0:T(8,128)(2,1)}, f32[3,2,512]{2,1,0:T(2,128)}) custom-call(s32[3,96]{1,0:T(4,128)} %mask_ref.1, bf16[12,3,256,256]{3,2,1,0:T(8,128)(2,1)} %bitcast.5, bf16[3,12,8,512]{3,2,1,0:T(8,128)(2,1)} %bitcast.7, f32[3,2,512]{2,1,0:T(2,128)} %dinv_ref.1), custom_call_target="tpu_custom_call" | custom-call | tf_op jit(solution)/shard_map/selected_inverse/pallas_call | solution.py:466
  140.2 1.7 %copy.9 = bf16[3,12,1,8,512]{4,3,2,1,0:T(8,128)(2,1)} copy(bf16[3,12,1,8,512]{4,3,2,1,0:T(8,128)(2,1)} %bitcast.6) | data formatting | bytes 589824
  141.9 1.3 copy.10

commit v2 on v0

v2 whole, which is shorter than its diff:
```python
import functools

import jax
import jax.numpy as jnp
from jax import lax
from jax.experimental import pallas as pl
from jax.experimental.pallas import tpu as pltpu
from jax.sharding import PartitionSpec as P

MESH = pl.DeviceIdType.MESH
F32 = jnp.float32
BF16 = jnp.bfloat16
I16 = jnp.int16
SUB = 8
LEVELS = 32000.0
PARTS = 2
LAG = 1
AHEAD = 2


def kernel(
    NP, NCOL, mask_ref, anc_ref, panel_ref, dinv_ref, col_ref, diag_ref,
    mfull, mf, sib, mpair, lbuf, cbuf, sbuf, rbuf, ysb, yrb, colp, perm, mpt,
    dsend, drecv, fsend, frecv, esend, erecv,
    m_l, m_s, m_r, a0_s, a0_r, a1_s, a1_r, l_s, a2_r, a3_r,
    r_s, r_r, y_s, y_r, c_s, c_r, d_s, d_r, f_s, f_r, e_s, e_r,
):
    SETS, RT, _, W = panel_ref.shape
    CT = anc_ref.shape[1]
    TILE = anc_ref.shape[-1]
    HALF = RT // 2
    NC = NCOL // 2
    Z = NC // 2
    NH = NCOL // NP
    WP = W // PARTS
    COUNT = SETS * PARTS
    LC = WP // 2
    WH = W // 2
    X = NP // 2
    NU = 4
    LONG = Z // 2
    SHORT = Z - 1 - LONG

    p = lax.axis_index("prow")
    q = lax.axis_index("pcol")
    core = lax.rem(q, 2)
    chip = q // 2
    z = lax.rem(chip, Z)
    yh = chip // Z
    sibling = (p, q + 1 - 2 * core)

    def at_chip(row, y, depth):
        return (row, (y * Z + depth) * 2 + core)

    u_me = lax.rem(p, 2) * 2 + yh

    def x_line(step):
        return at_chip(2 * lax.rem(p // 2 + step, X) + lax.rem(p, 2), yh, z)

    def y_line(step):
        other = lax.rem(u_me + step, NU)
        return at_chip(2 * (p // 2) + other // 2, lax.rem(other, 2), z)

    y_mate = at_chip(p, 1 - yh, z)

    def turn(depth):
        return lax.rem(depth, X) + (X // 2) * (depth // X)

    def held(row, depth, c):
        return c * Z + 2 * lax.rem(row // 2 + 2 * X - turn(depth), X) + lax.rem(row, 2)

    TWINS = 1
    mine = held(p, z, core)
    far = held(2 * lax.rem(p // 2 + X // 2, X) + lax.rem(p, 2), z, core)

    def a1_target(h2, twin):
        depth = h2 * X + p // 2
        row = 2 * lax.rem(z // 2 + turn(depth) + twin * (X // 2), X) + lax.rem(z, 2)
        return (row, (core * Z + depth) * 2 + yh)

    def a1_is_me(h2, twin):
        row, column = a1_target(h2, twin)
        return jnp.logical_and(row == p, column == q)

    def a1_source(half, twin):
        return (2 * lax.rem(z, X) + half, 2 * (far if twin else mine) + yh)

    def signal(where):
        pl.semaphore_signal(barrier, inc=1, device_id=where, device_id_type=MESH)

    barrier = pltpu.get_barrier_semaphore()
    signal(sibling)

    for step in range(1, X):
        signal(x_line(step))
    for step in range(1, NU):
        signal(y_line(step))

    @pl.loop(1, Z)
    def _(step):
        signal(at_chip(p, yh, lax.rem(z + step, Z)))

    expected = 1 + (X - 1) + (NU - 1) + (Z - 1)
    for twin in range(TWINS):
        for e in range(2):
            me = a1_is_me(e, twin)
            row, column = a1_source(e, twin)
            from_me = jnp.logical_and(row == p, column == q)

            @pl.when(jnp.logical_not(me))
            def _():
                signal(a1_target(e, twin))

            @pl.when(jnp.logical_not(from_me))
            def _():
                signal((row, column))

            expected = expected + jnp.where(me, 0, 1) + jnp.where(from_me, 0, 1)

    def copy(src, dst, send, recv, where):
        return pltpu.make_async_remote_copy(
            src_ref=src, dst_ref=dst, send_sem=send, recv_sem=recv,
            device_id=where, device_id_type=MESH,
        )

    def lanes(half, b):
        return pl.ds(pl.multiple_of((half * CT + b) * TILE, TILE), TILE)

    def m_local(b):
        return pltpu.make_async_copy(
            anc_ref.at[pl.ds(core * HALF, HALF), b], mfull.at[:, :, :, :, lanes(core, b)], m_l.at[b])

    def m_swap(b):
        return copy(
            anc_ref.at[pl.ds((1 - core) * HALF, HALF), b], mfull.at[:, :, :, :, lanes(core, b)],
            m_s.at[0], m_r.at[0], sibling)

    for b in range(CT):
        m_local(b).start()

    def keep(s, a):
        return mask_ref[s, a * NP + p].astype(F32)

    @pl.loop(0, SETS)
    def _(s):
        @pl.loop(0, RT)
        def _(a):
            mf[s, a] = panel_ref[s, a].astype(F32) * keep(s, a)

    rows = lax.broadcasted_iota(jnp.int32, (WH, W), 0)
    columns = lax.broadcasted_iota(jnp.int32, (WH, W), 1)
    hit = columns == (rows >> 1) * 4 + 2 * core + (rows & 1)
    perm[...] = jnp.where(hit, 1.0, 0.0).astype(BF16)

    pl.semaphore_wait(barrier, expected)

    def a0(s):
        return copy(mf.at[s], sib.at[s], a0_s.at[0], a0_r.at[s], sibling)

    for s in range(SETS):
        a0(s).start()
    for b in range(CT):
        m_swap(b).start()

    def l_slice(n, index):
        return lbuf.at[n, :, pl.ds(pl.multiple_of(16 * index, 16), 16), :]

    def l_bytes(n, count):
        return lbuf.at[n, :, pl.ds(0, 16 * count), :]

    def l_all(count):
        return lbuf.at[:, :, pl.ds(0, 16 * count), :]

    def a1_dst(s):
        return lbuf.at[
            pl.ds(s * PARTS, PARTS), pl.ds(lax.rem(p, 2) * CT, CT),
            pl.ds(pl.multiple_of(16 * chip, 16), 16), :]

    def a1(s, h2, twin):
        return copy(
            mpair.at[s, :, :, 2 * core + h2], a1_dst(s), a1_s.at[s, h2, twin], a1_r.at[s, twin],
            a1_target(h2, twin))

    def a1_local(s, h2, twin):
        return pltpu.make_async_copy(mpair.at[s, :, :, 2 * core + h2], a1_dst(s), a1_r.at[s, twin])

    def a1_wait(s, twin):
        index = far if twin else mine
        got = lbuf.at[pl.ds(s * PARTS, PARTS), :, pl.ds(pl.multiple_of(16 * index, 16), 16), :]
        copy(got, got, a1_s.at[s, 0, twin], a1_r.at[s, twin], sibling).wait_recv()

    @pl.loop(0, SETS)
    def _(s):
        a0(s).wait_recv()
        own = mf[s]
        other = sib[s]
        low = jnp.where(core == 0, own, other)
        high = jnp.where(core == 0, other, own)
        both = jnp.concatenate([low, high], axis=1).astype(BF16).reshape(CT, NH, 16, W)
        for w in range(PARTS):
            mpair[s, w] = both[..., w * WP : (w + 1) * WP]
        for twin in range(TWINS):
            for h2 in range(2):
                me = a1_is_me(h2, twin)

                @pl.when(me)
                def _():
                    a1_local(s, h2, twin).start()

                @pl.when(jnp.logical_not(me))
                def _():
                    a1(s, h2, twin).start()

    def transposed(s):
        total = jnp.zeros((WH, RT * 16), F32)
        for w in range(PARTS):
            total = total + lax.dot_general(
                perm[:, w * WP : (w + 1) * WP], mpair[s, w].reshape(RT * 16, WP),
                (((1,), (1,)), ((), ())), preferred_element_type=F32)
        mpt[s] = total.astype(BF16)

    def along(dx):
        return (2 * lax.rem(p // 2 + dx, X) + lax.rem(p, 2), q)

    over = (p + 1 - 2 * lax.rem(p, 2), q)

    def origin(step):
        row = lax.rem(p // 2 + X - step // 2, X)
        return held(2 * row + lax.rem(lax.rem(p, 2) + step, 2), z, core)

    def a2_over(n):
        return copy(l_slice(n, mine), l_slice(n, mine), l_s.at[0], a2_r.at[n, 1], over)

    def a2_over_far(n):
        return copy(l_slice(n, far), l_slice(n, far), l_s.at[0], a2_r.at[n, X + 1], over)

    NEAR = [dx for dx in range(1, X) if TWINS == 1 or dx != X // 2]
    LATER = [step for step in range(2, NP) if TWINS == 1 or step != X]

    def a2(n, dx, dy):
        index = mine if dy == 0 else held(over[0], z, core)
        return copy(l_slice(n, index), l_slice(n, index), l_s.at[0], a2_r.at[n, 2 * dx + dy], along(dx))

    def a2_wait(n, step):
        copy(l_slice(n, mine), l_slice(n, mine), l_s.at[0], a2_r.at[n, step], sibling).wait_recv()

    def a2_sibling(n):
        return copy(l_slice(n, mine), l_slice(n, mine), l_s.at[0], a3_r.at[n], sibling)

    def a3(n, step):
        index = origin(step)
        return copy(l_slice(n, index), l_slice(n, index), l_s.at[0], a3_r.at[n], sibling)

    def spread(n):
        @pl.when(lax.rem(n, PARTS) == 0)
        def _():
            a1_wait(n // PARTS, 0)

        a2_over(n).start()
        for dx in NEAR:
            a2(n, dx, 0).start()

        a2_sibling(n).start()
        if TWINS == 2:
            @pl.when(lax.rem(n, PARTS) == 0)
            def _():
                a1_wait(n // PARTS, 1)

            a2_over_far(n).start()
            a3(n, X).start()

    def relay(n):
        a2_wait(n, 1)
        for dx in NEAR:
            a2(n, dx, 1).start()

        a3(n, 1).start()

    @pl.loop(0, AHEAD)
    def _(n):
        spread(n)

    relay(0)

    def piece(n, depth, j):
        return (n, slice(None), slice(None), depth, slice(None), pl.ds(j * LC, LC))

    def y_piece(n, y, j):
        return (n, slice(None), y, z, slice(None), pl.ds(j * LC, LC))

    def pack(index, dst, count):
        groups = count // SUB
        top = jnp.zeros((SUB, LC), F32)
        for j in range(2):
            v = cbuf[index(j)].reshape(groups, SUB, LC)
            top = jnp.maximum(top, jnp.max(jnp.abs(v), axis=0))
        power = jnp.minimum(jnp.maximum(jnp.ceil(jnp.log2(top)), -100.0), 100.0)
        factor = jnp.exp2(-power) * LEVELS
        for j in range(2):
            v = cbuf[index(j)].reshape(groups, SUB, LC) * factor[None]
            whole = jnp.round(v).astype(jnp.int32).astype(I16)
            dst[pl.ds(j * count, count), :] = whole.reshape(count, LC)
        power = power.astype(jnp.int32)
        dst[pl.ds(2 * count, 16), :] = jnp.concatenate([power, power], axis=0).astype(I16)

    def scale_of(src, count):
        power = src[pl.ds(2 * count, 16), :].astype(jnp.int32).astype(F32)[:SUB]
        return jnp.exp2(power) * (1.0 / LEVELS)

    def unpack(src, scale, j, count):
        v = src[pl.ds(j * count, count), :].astype(jnp.int32).astype(F32)
        return v.reshape(count // SUB, SUB, LC) * scale[None]

    RING = HALF * 2 * 16
    MATE = HALF * 16

    def arm(n, way):
        return jnp.where(lax.rem(n, 2) == way, LONG, SHORT)

    def hop(n, way, k):
        step = 1 if way == 0 else Z - 1
        where = at_chip(p, yh, lax.rem(z + step, Z))
        slot = jnp.where(lax.rem(n, 2) == way, k, LONG + k)
        return copy(sbuf.at[n, slot], rbuf.at[n, slot], r_s.at[0], r_r.at[n, slot], where)

    def multiply(n, depth):
        product = jnp.dot(
            mfull[:, :, depth].reshape(RING, 2 * CT * TILE), lbuf[n].reshape(2 * CT * TILE, WP),
            preferred_element_type=F32)
        cbuf[n, :, :, depth] = product.reshape(HALF, 2, 16, WP)

    def ring_step(n, way, k):
        length = arm(n, way)
        left = length - k
        depth = lax.rem(z + Z + (left if way == 0 else -left), Z)

        @pl.when(k < length)
        def _():
            multiply(n, depth)

        @pl.when(jnp.logical_and(k > 0, k <= length))
        def _():
            hop(n, way, k - 1).wait_recv()
            src = rbuf.at[n, jnp.where(lax.rem(n, 2) == way, k - 1, LONG + k - 1)]
            scale = scale_of(src, RING)
            for j in range(2):
                index = piece(n, depth, j)
                shape = (HALF, 2, 16, LC)
                cbuf[index] = cbuf[index] + unpack(src, scale, j, RING).reshape(shape)

        @pl.when(k < length)
        def _():
            slot = jnp.where(lax.rem(n, 2) == way, k, LONG + k)
            pack(lambda j: piece(n, depth, j), sbuf.at[n, slot], RING)
            hop(n, way, k).start()

    def y_copy(n):
        return copy(ysb.at[n], yrb.at[n], y_s.at[0], y_r.at[n], y_mate)

    def c_copy(n):
        return copy(colp.at[n, core], colp.at[n, core], c_s.at[0], c_r.at[n], sibling)

    def arrive(n):
        @pl.when(n + 1 < COUNT)
        def _():
            relay(n + 1)

        @pl.when(n + AHEAD < COUNT)
        def _():
            spread(n + AHEAD)

        for step in LATER:
            a2_wait(n, step)
            a3(n, step).start()

        copy(l_bytes(n, NP), l_bytes(n, NP), l_s.at[0], a3_r.at[n], sibling).wait_recv()

        @pl.when(n == 0)
        def _():
            for s in range(SETS):
                transposed(s)

            for b in range(CT):
                m_local(b).wait()
            other = mfull.at[:, :, :, :, pl.ds(0, CT * TILE)]
            copy(other, other, m_s.at[0], m_r.at[0], sibling).wait_recv()

    def y_arrive(n):
        y_copy(n).wait_recv()
        src = yrb.at[n]
        scale = scale_of(src, MATE)
        for j in range(2):
            total = cbuf[y_piece(n, yh, j)] + unpack(src, scale, j, MATE).reshape(HALF, 16, LC)
            for a in range(HALF):
                image = -total[a] * keep(n // PARTS, core * HALF + a)
                colp[n, core, a, :, pl.ds(j * LC, LC)] = image.astype(BF16)
        c_copy(n).start()

    def d_copy(n, step):
        other = lax.rem(p // 2 + step, X)
        return copy(dsend.at[n, other], drecv.at[n, step], d_s.at[0], d_r.at[n], x_line(step))

    def f_copy(n, step):
        other = lax.rem(u_me + step, NU)
        return copy(fsend.at[n, other], frecv.at[n, step], f_s.at[0], f_r.at[n], y_line(step))

    def part_lanes(n):
        return pl.ds(pl.multiple_of(lax.rem(n, PARTS) * WP, WP), WP)

    def c_arrive(n):
        c_copy(n).wait_recv()
        dsend[n] = jnp.dot(
            mpt[n // PARTS], colp[n].reshape(RT * 16, WP), preferred_element_type=F32
        ).reshape(X, NU, 2 * Z, WP)
        for step in range(1, X):
            d_copy(n, step).start()

        both = colp[n].reshape(RT, 16, WP).astype(F32)
        picked = jnp.where(core == 0, both[:, :SUB], both[:, SUB:])
        col_ref[n // PARTS, :, :, part_lanes(n)] = picked.astype(BF16)

    def d_arrive(n):
        total = dsend[n, p // 2]
        if X > 1:
            got = drecv.at[n, pl.ds(1, X - 1)]
            copy(got, got, d_s.at[0], d_r.at[n], sibling).wait_recv()
            for step in range(1, X):
                total = total + drecv[n, step]
        fsend[n] = total
        for step in range(1, NU):
            f_copy(n, step).start()

    def f_arrive(n):
        got = frecv.at[n, pl.ds(1, NU - 1)]
        copy(got, got, f_s.at[0], f_r.at[n], sibling).wait_recv()
        total = fsend[n, u_me]
        for step in range(1, NU):
            total = total + frecv[n, step]
        for depth in range(Z):
            esend[depth, n // PARTS, :, part_lanes(n)] = total[2 * depth : 2 * depth + 2]

    @pl.loop(0, (COUNT - 1) * LAG + LONG + 5)
    def _(t):
        @pl.loop(0, COUNT)
        def _(n):
            k = t - n * LAG

            @pl.when(jnp.logical_and(k >= 1, k <= LONG))
            def _():
                for way in range(2):
                    ring_step(n, way, k)

            @pl.when(k == LONG)
            def _():
                pack(lambda j: y_piece(n, 1 - yh, j), ysb.at[n], MATE)
                y_copy(n).start()

        @pl.loop(0, COUNT)
        def _(n):
            k = t - n * LAG

            @pl.when(k == LONG + 4)
            def _():
                f_arrive(n)

            @pl.when(k == LONG + 3)
            def _():
                d_arrive(n)

            @pl.when(k == LONG + 2)
            def _():
                c_arrive(n)

            @pl.when(k == LONG + 1)
            def _():
                y_arrive(n)

            @pl.when(k == 0)
            def _():
                arrive(n)
                for way in range(2):
                    ring_step(n, way, k)
                multiply(n, z)

    def e_copy(step):
        other = lax.rem(z + step, Z)
        return copy(esend.at[other], erecv.at[step], e_s.at[0], e_r.at[0], at_chip(p, yh, other))

    @pl.loop(1, Z)
    def _(step):
        e_copy(step).start()

    got = erecv.at[pl.ds(1, Z - 1)]
    copy(got, got, e_s.at[0], e_r.at[0], sibling).wait_recv()
    total = esend[z]
    for step in range(1, Z):
        total = total + erecv[step]
    diag_ref[...] = dinv_ref[...] - total

    def sent(what, sem):
        copy(what, what, sem.at[0], sem.at[0], sibling).wait_send()

    sent(mfull.at[:, :, :, :, pl.ds(0, CT * TILE)], m_s)
    sent(mf, a0_s)
    sent(l_all(2 * NP - TWINS), l_s)
    sent(sbuf, r_s)
    sent(ysb, y_s)
    sent(colp.at[:, 0], c_s)
    if X > 1:
        sent(dsend.at[:, pl.ds(1, X - 1)], d_s)
    sent(fsend.at[:, pl.ds(1, NU - 1)], f_s)
    sent(got, e_s)

    @pl.loop(0, SETS)
    def _(s):
        for h2 in range(2):
            for twin in range(TWINS):
                @pl.when(jnp.logical_not(a1_is_me(h2, twin)))
                def _():
                    a1(s, h2, twin).wait_send()


def body(anc_inverse, panel, tile_mask, diag_inverse):
    n_row = lax.axis_size("prow")
    n_col = lax.axis_size("pcol")
    sets, rt, _, sub, w = panel.shape
    _, tile, ct, _ = anc_inverse.shape
    nz = n_col // 4
    anc = jnp.transpose(anc_inverse, (0, 2, 1, 3)).reshape(rt, ct, 2, nz, 16, tile)
    slim = panel.reshape(sets, rt, sub, w)
    half, nz, nh = rt // 2, n_col // 4, n_col // n_row
    wp, count = w // PARTS, sets * PARTS
    lc = wp // 2
    hops = nz - 1
    message = 2 * half * 2 * 16 + 16
    mate = 2 * half * 16 + 16
    dma = pltpu.SemaphoreType.DMA
    vmem = pl.BlockSpec(memory_space=pltpu.VMEM)
    scratch = [
        pltpu.VMEM((half, 2, nz, 16, 2 * ct * tile), BF16),
        pltpu.VMEM((sets, rt, sub, w), F32),
        pltpu.VMEM((sets, rt, sub, w), F32),
        pltpu.VMEM((sets, PARTS, ct, nh, 16, wp), BF16),
        pltpu.VMEM((count, 2 * ct, tile, wp), BF16),
        pltpu.VMEM((count, half, 2, nz, 16, wp), F32),
        pltpu.VMEM((count, hops, message, lc), I16),
        pltpu.VMEM((count, hops, message, lc), I16),
        pltpu.VMEM((count, mate, lc), I16),
        pltpu.VMEM((count, mate, lc), I16),
        pltpu.VMEM((count, 2, half, 16, wp), BF16),
        pltpu.VMEM((w // 2, w), BF16),
        pltpu.VMEM((sets, w // 2, rt * 16), BF16),
        pltpu.VMEM((count, n_row // 2, 4, 2 * nz, wp), F32),
        pltpu.VMEM((count, n_row // 2, 4, 2 * nz, wp), F32),
        pltpu.VMEM((count, 4, 2 * nz, wp), F32),
        pltpu.VMEM((count, 4, 2 * nz, wp), F32),
        pltpu.VMEM((nz, sets, 2, w), F32),
        pltpu.VMEM((nz, sets, 2, w), F32),
        dma((ct,)), dma((1,)), dma((1,)),
        dma((1,)), dma((sets,)),
        dma((sets, 2, 2)), dma((sets, 2)),
        dma((1,)), dma((count, n_row)), dma((count,)),
        dma((1,)), dma((count, hops)),
        dma((1,)), dma((count,)),
        dma((1,)), dma((count,)),
        dma((1,)), dma((count,)),
        dma((1,)), dma((count,)),
        dma((1,)), dma((1,)),
    ]
    column, diag = pl.pallas_call(
        functools.partial(kernel, n_row, n_col),
        out_shape=(
            jax.ShapeDtypeStruct((sets, rt, sub, w), BF16),
            jax.ShapeDtypeStruct(diag_inverse.shape, F32),
        ),
        in_specs=[
            pl.BlockSpec(memory_space=pltpu.SMEM),
            pl.BlockSpec(memory_space=pl.ANY),
            vmem,
            vmem,
        ],
        out_specs=(vmem, vmem),
        scratch_shapes=scratch,
        compiler_params=pltpu.CompilerParams(
            collective_id=0, has_side_effects=True, vmem_limit_bytes=56 * 1024 * 1024
        ),
        name="selected_inverse",
    )(tile_mask, anc, slim, diag_inverse)
    return column.reshape(panel.shape), diag


def solution(mesh):
    in_specs = (
        P(None, "prow", None, "pcol"),
        P(None, None, "prow", "pcol", None),
        P(),
        P(None, ("prow", "pcol"), None),
    )
    out_specs = (P(None, None, "prow", "pcol", None), P(None, ("prow", "pcol"), None))
    return jax.shard_map(body, mesh=mesh, in_specs=in_specs, out_specs=out_specs, check_vma=False)
```

time: 1120 us -> 129 us (0.12)
  waiting for transfers between devices: 987 us -> 0 us
  Pallas kernels: 0 us -> 125 us
  local copies, waits for them, and re-layouts: 59.3 us -> 3 us
  starting transfers between devices: 24.5 us -> 0 us
  matrix products: 23.9 us -> 0 us
  between operations: 14.6 us -> 0.64 us
    unnamed x7 -> x0, waiting for transfers between devices: 806 us -> none
    pallas_call x0 -> x1, Pallas kernels: none -> 125 us  [body(): pl.pallas_call(functools.partial(kernel, n_row, n_col), out_shape=(jax.Sh...]
    psum x1 -> x0, waiting for transfers between devices: 117 us -> none  [spread(): return lax.psum(jnp.where(mine, x, jnp.zeros_like(x)), axis)]
    all_to_all x3 -> x0, waiting for transfers between devices: 64.4 us -> none  [body(): lax.all_to_all(outgoing[index:index + 1], 'pcol', split_axis=2, concat_ax...]
    transpose x3 -> x0, local copies, waits for them, and re-layouts: 48.2 us -> none  [local_product(): jnp.einsum('aibj,sbjw->isaw', anc_block, columns, preferred_element_type=...]
    all_to_all x3 -> x0, starting transfers between devices: 24.4 us -> none  [body(): lax.all_to_all(outgoing[index:index + 1], 'pcol', split_axis=2, concat_ax...]
    dot_general x4 -> x0, matrix products: 23.9 us -> none  [the longest x3 21.6 us: local_product(): jnp.einsum('aibj,sbjw->isaw', anc_block, columns, preferred_element_type=...]
  transfers between devices with their start and end apart: 7 -> 0, of which waited for: 7 -> 0; matrix products, arithmetic and copies ran while one was open for 5% -> 0% of each run, Pallas kernels for 0% -> 0%
where the time goes in v2:
time: 129 us
  Pallas kernels  125 us (97%)
  local copies, waits for them, and re-layouts  3 us (2%)
    pallas_call x1, Pallas kernels, body(): pl.pallas_call(functools.partial(kernel, n_row, n_col), out_shape=(jax.Sh...  125 us
    unnamed x2, local copies, waits for them, and re-layouts  3 us

profile of v2, /device:TPU:24, one launch (start us, length us, event | category | flops | bytes accessed | tf_op | source)
XLA Modules:
  0.0 128.5 jit_solution(5243119448003211573)
XLA Ops:
  0.6 124.9 %selected_inverse.1 = (bf16[3,12,8,512]{3,2,1,0:T(8,128)(2,1)}, f32[3,2,512]{2,1,0:T(2,128)}) custom-call(s32[3,96]{1,0:T(4,128)} %mask_ref.1, bf16[12,3,2,8,16,256]{5,4,3,2,1,0:T(8,128)(2,1)} %bitcast.7, bf16[3,12,8,512]{3,2,1,0:T(8,128)(2,1)} %bitcast.9, f32[3,2,512]{2,1,0:T(2,128)} %dinv_ref.1), custom_call_target="tpu_custom_call" | custom-call | tf_op jit(solution)/shard_map/selected_inverse/pallas_call | solution.py:570
  125.5 1.7 %copy.9 = bf16[3,12,1,8,512]{4,3,2,1,0:T(8,128)(2,1)} copy(bf16[3,12,1,8,512]{4,3,2,1,0:T(8,128)(2,1)} %bitcast.8) | data formatting | bytes 589824
  127.2 1.3 %copy.10 = f32[3,2,512]{2,1,0:T(2,128)} copy(f32[3,2,512]{2,1,0:T(2,128)} %get-tuple-element.11) | data formatting | bytes 24576

commit v3 on v2

--- a/solution.py
+++ b/solution.py
@@ -95,12 +95,15 @@
         signal(x_line(step))
     for step in range(1, NU):
         signal(y_line(step))
+    for step in range(3, NP, 2):
+        signal((2 * lax.rem(p // 2 + step // 2, X) + lax.rem(p + 1, 2), q))
+
 
     @pl.loop(1, Z)
     def _(step):
         signal(at_chip(p, yh, lax.rem(z + step, Z)))
 
-    expected = 1 + (X - 1) + (NU - 1) + (Z - 1)
+    expected = 1 + 2 * (X - 1) + (NU - 1) + (Z - 1)
     for twin in range(TWINS):
         for e in range(2):
             me = a1_is_me(e, twin)
@@ -219,27 +222,15 @@
                 (((1,), (1,)), ((), ())), preferred_element_type=F32)
         mpt[s] = total.astype(BF16)
 
-    def along(dx):
-        return (2 * lax.rem(p // 2 + dx, X) + lax.rem(p, 2), q)
-
-    over = (p + 1 - 2 * lax.rem(p, 2), q)
+    def across(step):
+        return (2 * lax.rem(p // 2 + step // 2, X) + lax.rem(p + step, 2), q)
 
     def origin(step):
         row = lax.rem(p // 2 + X - step // 2, X)
-        return held(2 * row + lax.rem(lax.rem(p, 2) + step, 2), z, core)
-
-    def a2_over(n):
-        return copy(l_slice(n, mine), l_slice(n, mine), l_s.at[0], a2_r.at[n, 1], over)
-
-    def a2_over_far(n):
-        return copy(l_slice(n, far), l_slice(n, far), l_s.at[0], a2_r.at[n, X + 1], over)
-
-    NEAR = [dx for dx in range(1, X) if TWINS == 1 or dx != X // 2]
-    LATER = [step for step in range(2, NP) if TWINS == 1 or step != X]
-
-    def a2(n, dx, dy):
-        index = mine if dy == 0 else held(over[0], z, core)
-        return copy(l_slice(n, index), l_slice(n, index), l_s.at[0], a2_r.at[n, 2 * dx + dy], along(dx))
+        return held(2 * row + lax.rem(p + step, 2), z, core)
+
+    def a2(n, step):
+        return copy(l_slice(n, mine), l_slice(n, mine), l_s.at[0], a2_r.at[n, step], across(step))
 
     def a2_wait(n, step):
         copy(l_slice(n, mine), l_slice(n, mine), l_s.at[0], a2_r.at[n, step], sibling).wait_recv()
@@ -256,31 +247,14 @@
         def _():
             a1_wait(n // PARTS, 0)
 
-        a2_over(n).start()
-        for dx in NEAR:
-            a2(n, dx, 0).start()
+        for step in range(1, NP):
+            a2(n, step).start()
 
         a2_sibling(n).start()
-        if TWINS == 2:
-            @pl.when(lax.rem(n, PARTS) == 0)
-            def _():
-                a1_wait(n // PARTS, 1)
-
-            a2_over_far(n).start()
-            a3(n, X).start()
-
-    def relay(n):
-        a2_wait(n, 1)
-        for dx in NEAR:
-            a2(n, dx, 1).start()
-
-        a3(n, 1).start()
 
     @pl.loop(0, AHEAD)
     def _(n):
         spread(n)
-
-    relay(0)
 
     def piece(n, depth, j):
         return (n, slice(None), slice(None), depth, slice(None), pl.ds(j * LC, LC))
@@ -361,25 +335,18 @@
         return copy(colp.at[n, core], colp.at[n, core], c_s.at[0], c_r.at[n], sibling)
 
     def arrive(n):
-        @pl.when(n + 1 < COUNT)
-        def _():
-            relay(n + 1)
+        for step in range(1, NP):
+            a2_wait(n, step)
+            a3(n, step).start()
 
         @pl.when(n + AHEAD < COUNT)
         def _():
             spread(n + AHEAD)
 
-        for step in LATER:
-            a2_wait(n, step)
-            a3(n, step).start()
-
         copy(l_bytes(n, NP), l_bytes(n, NP), l_s.at[0], a3_r.at[n], sibling).wait_recv()
 
         @pl.when(n == 0)
         def _():
-            for s in range(SETS):
-                transposed(s)
-
             for b in range(CT):
                 m_local(b).wait()
             other = mfull.at[:, :, :, :, pl.ds(0, CT * TILE)]
@@ -481,6 +448,11 @@
                 for way in range(2):
                     ring_step(n, way, k)
                 multiply(n, z)
+
+                @pl.when(n == 0)
+                def _():
+                    for s in range(SETS):
+                        transposed(s)
 
     def e_copy(step):
         other = lax.rem(z + step, Z)

time: 129 us -> 126 us (0.977)
  Pallas kernels: 125 us -> 122 us
    pallas_call x1, Pallas kernels: 125 us -> 122 us  [body(): pl.pallas_call(functools.partial(kernel, n_row, n_col), out_shape=(jax.Sh...]
where the time goes in v3:
time: 126 us
  Pallas kernels  122 us (97%)
  local copies, waits for them, and re-layouts  3 us (2%)
    pallas_call x1, Pallas kernels, body(): pl.pallas_call(functools.partial(kernel, n_row, n_col), out_shape=(jax.Sh...  122 us
    unnamed x2, local copies, waits for them, and re-layouts  3 us

profile of v3, /device:TPU:24, one launch (start us, length us, event | category | flops | bytes accessed | tf_op | source)
XLA Modules:
  0.0 125.7 jit_solution(10785606579976088861)
XLA Ops:
  0.6 122.0 %selected_inverse.1 = (bf16[3,12,8,512]{3,2,1,0:T(8,128)(2,1)}, f32[3,2,512]{2,1,0:T(2,128)}) custom-call(s32[3,96]{1,0:T(4,128)} %mask_ref.1, bf16[12,3,2,8,16,256]{5,4,3,2,1,0:T(8,128)(2,1)} %bitcast.7, bf16[3,12,8,512]{3,2,1,0:T(8,128)(2,1)} %bitcast.9, f32[3,2,512]{2,1,0:T(2,128)} %dinv_ref.1), custom_call_target="tpu_custom_call" | custom-call | tf_op jit(solution)/shard_map/selected_inverse/pallas_call | solution.py:542
  122.7 1.7 %copy.9 = bf16[3,12,1,8,512]{4,3,2,1,0:T(8,128)(2,1)} copy(bf16[3,12,1,8,512]{4,3,2,1,0:T(8,128)(2,1)} %bitcast.8) | data formatting | bytes 589824
  124.4 1.3 %copy.10 = f32[3,2,512]{2,1,0:T(2,128)} copy(f32[3,2,512]{2,1,0:T(2,128)} %get-tuple-element.11) | data formatting | bytes 24576

commit v4 on v3

--- a/solution.py
+++ b/solution.py
@@ -242,12 +242,15 @@
         index = origin(step)
         return copy(l_slice(n, index), l_slice(n, index), l_s.at[0], a3_r.at[n], sibling)
 
+    FAR = [step for step in range(1, NP) if X > 1 and step // 2 == X // 2]
+    CLOSE = [step for step in range(1, NP) if step not in FAR]
+
     def spread(n):
         @pl.when(lax.rem(n, PARTS) == 0)
         def _():
             a1_wait(n // PARTS, 0)
 
-        for step in range(1, NP):
+        for step in FAR + CLOSE[1:] + CLOSE[:1]:
             a2(n, step).start()
 
         a2_sibling(n).start()
@@ -335,7 +338,7 @@
         return copy(colp.at[n, core], colp.at[n, core], c_s.at[0], c_r.at[n], sibling)
 
     def arrive(n):
-        for step in range(1, NP):
+        for step in CLOSE + FAR:
             a2_wait(n, step)
             a3(n, step).start()
 

time: 126 us -> 125 us (level)
  no operation moved by 1% of the time
where the time goes in v4:
time: 125 us
  Pallas kernels  121 us (97%)
  local copies, waits for them, and re-layouts  3 us (2%)
    pallas_call x1, Pallas kernels, body(): pl.pallas_call(functools.partial(kernel, n_row, n_col), out_shape=(jax.Sh...  121 us
    unnamed x2, local copies, waits for them, and re-layouts  3 us

profile of v4, /device:TPU:24, one launch (start us, length us, event | category | flops | bytes accessed | tf_op | source)
XLA Modules:
  0.0 125.1 jit_solution(510339959465677510)
XLA Ops:
  0.6 121.5 %selected_inverse.1 = (bf16[3,12,8,512]{3,2,1,0:T(8,128)(2,1)}, f32[3,2,512]{2,1,0:T(2,128)}) custom-call(s32[3,96]{1,0:T(4,128)} %mask_ref.1, bf16[12,3,2,8,16,256]{5,4,3,2,1,0:T(8,128)(2,1)} %bitcast.7, bf16[3,12,8,512]{3,2,1,0:T(8,128)(2,1)} %bitcast.9, f32[3,2,512]{2,1,0:T(2,128)} %dinv_ref.1), custom_call_target="tpu_custom_call" | custom-call | tf_op jit(solution)/shard_map/selected_inverse/pallas_call | solution.py:545
  122.1 1.7 %copy.9 = bf16[3,12,1,8,512]{4,3,2,1,0:T(8,128)(2,1)} copy(bf16[3,12,1,8,512]{4,3,2,1,0:T(8,128)(2,1)} %bitcast.8) | data formatting | bytes 589824
  123.8 1.3 %copy.10 = f32[3,2,512]{2,1,0:T(2,128)} copy(f32[3,2,512]{2,1,0:T(2,128)} %get-tuple-element.11) | data formatting | bytes 24576

commit v5 on v4

--- a/solution.py
+++ b/solution.py
@@ -62,6 +62,7 @@
         return at_chip(2 * (p // 2) + other // 2, lax.rem(other, 2), z)
 
     y_mate = at_chip(p, 1 - yh, z)
+    y_cross = (p, ((1 - yh) * Z + z) * 2 + 1 - core)
 
     def turn(depth):
         return lax.rem(depth, X) + (X // 2) * (depth // X)
@@ -90,6 +91,7 @@
 
     barrier = pltpu.get_barrier_semaphore()
     signal(sibling)
+    signal(y_cross)
 
     for step in range(1, X):
         signal(x_line(step))
@@ -103,7 +105,7 @@
     def _(step):
         signal(at_chip(p, yh, lax.rem(z + step, Z)))
 
-    expected = 1 + 2 * (X - 1) + (NU - 1) + (Z - 1)
+    expected = 2 + 2 * (X - 1) + (NU - 1) + (Z - 1)
     for twin in range(TWINS):
         for e in range(2):
             me = a1_is_me(e, twin)
@@ -162,8 +164,6 @@
 
     for s in range(SETS):
         a0(s).start()
-    for b in range(CT):
-        m_swap(b).start()
 
     def l_slice(n, index):
         return lbuf.at[n, :, pl.ds(pl.multiple_of(16 * index, 16), 16), :]
@@ -254,6 +254,9 @@
             a2(n, step).start()
 
         a2_sibling(n).start()
+
+    for b in range(CT):
+        m_swap(b).start()
 
     @pl.loop(0, AHEAD)
     def _(n):
@@ -331,11 +334,13 @@
             pack(lambda j: piece(n, depth, j), sbuf.at[n, slot], RING)
             hop(n, way, k).start()
 
-    def y_copy(n):
-        return copy(ysb.at[n], yrb.at[n], y_s.at[0], y_r.at[n], y_mate)
+    def y_copy(n, cross):
+        return copy(
+            ysb.at[n, 0], yrb.at[n, cross], y_s.at[cross], y_r.at[n, cross],
+            y_cross if cross else y_mate)
 
     def c_copy(n):
-        return copy(colp.at[n, core], colp.at[n, core], c_s.at[0], c_r.at[n], sibling)
+        return copy(ysb.at[n, 1], yrb.at[n, 2], c_s.at[0], c_r.at[n], sibling)
 
     def arrive(n):
         for step in CLOSE + FAR:
@@ -356,15 +361,20 @@
             copy(other, other, m_s.at[0], m_r.at[0], sibling).wait_recv()
 
     def y_arrive(n):
-        y_copy(n).wait_recv()
-        src = yrb.at[n]
-        scale = scale_of(src, MATE)
-        for j in range(2):
-            total = cbuf[y_piece(n, yh, j)] + unpack(src, scale, j, MATE).reshape(HALF, 16, LC)
-            for a in range(HALF):
-                image = -total[a] * keep(n // PARTS, core * HALF + a)
-                colp[n, core, a, :, pl.ds(j * LC, LC)] = image.astype(BF16)
-        c_copy(n).start()
+        c_copy(n).wait_recv()
+        for cross in range(2):
+            y_copy(n, cross).wait_recv()
+        for cross in range(2):
+            near = yrb.at[n, 2] if cross else ysb.at[n, 1]
+            away = yrb.at[n, cross]
+            half = 1 - core if cross else core
+            near_scale, away_scale = scale_of(near, MATE), scale_of(away, MATE)
+            for j in range(2):
+                total = unpack(near, near_scale, j, MATE) + unpack(away, away_scale, j, MATE)
+                total = total.reshape(HALF, 16, LC)
+                for a in range(HALF):
+                    image = -total[a] * keep(n // PARTS, half * HALF + a)
+                    colp[n, half, a, :, pl.ds(j * LC, LC)] = image.astype(BF16)
 
     def d_copy(n, step):
         other = lax.rem(p // 2 + step, X)
@@ -378,7 +388,6 @@
         return pl.ds(pl.multiple_of(lax.rem(n, PARTS) * WP, WP), WP)
 
     def c_arrive(n):
-        c_copy(n).wait_recv()
         dsend[n] = jnp.dot(
             mpt[n // PARTS], colp[n].reshape(RT * 16, WP), preferred_element_type=F32
         ).reshape(X, NU, 2 * Z, WP)
@@ -409,7 +418,7 @@
         for depth in range(Z):
             esend[depth, n // PARTS, :, part_lanes(n)] = total[2 * depth : 2 * depth + 2]
 
-    @pl.loop(0, (COUNT - 1) * LAG + LONG + 5)
+    @pl.loop(0, (COUNT - 1) * LAG + LONG + 4)
     def _(t):
         @pl.loop(0, COUNT)
         def _(n):
@@ -422,28 +431,28 @@
 
             @pl.when(k == LONG)
             def _():
-                pack(lambda j: y_piece(n, 1 - yh, j), ysb.at[n], MATE)
-                y_copy(n).start()
+                pack(lambda j: y_piece(n, 1 - yh, j), ysb.at[n, 0], MATE)
+                for cross in range(2):
+                    y_copy(n, cross).start()
+                pack(lambda j: y_piece(n, yh, j), ysb.at[n, 1], MATE)
+                c_copy(n).start()
 
         @pl.loop(0, COUNT)
         def _(n):
             k = t - n * LAG
 
-            @pl.when(k == LONG + 4)
+            @pl.when(k == LONG + 3)
             def _():
                 f_arrive(n)
 
-            @pl.when(k == LONG + 3)
+            @pl.when(k == LONG + 2)
             def _():
                 d_arrive(n)
 
-            @pl.when(k == LONG + 2)
-            def _():
+            @pl.when(k == LONG + 1)
+            def _():
+                y_arrive(n)
                 c_arrive(n)
-
-            @pl.when(k == LONG + 1)
-            def _():
-                y_arrive(n)
 
             @pl.when(k == 0)
             def _():
@@ -479,8 +488,9 @@
     sent(mf, a0_s)
     sent(l_all(2 * NP - TWINS), l_s)
     sent(sbuf, r_s)
-    sent(ysb, y_s)
-    sent(colp.at[:, 0], c_s)
+    for cross in range(2):
+        copy(ysb.at[:, 0], ysb.at[:, 0], y_s.at[cross], y_s.at[cross], sibling).wait_send()
+    sent(ysb.at[:, 1], c_s)
     if X > 1:
         sent(dsend.at[:, pl.ds(1, X - 1)], d_s)
     sent(fsend.at[:, pl.ds(1, NU - 1)], f_s)
@@ -520,8 +530,8 @@
         pltpu.VMEM((count, half, 2, nz, 16, wp), F32),
         pltpu.VMEM((count, hops, message, lc), I16),
         pltpu.VMEM((count, hops, message, lc), I16),
-        pltpu.VMEM((count, mate, lc), I16),
-        pltpu.VMEM((count, mate, lc), I16),
+        pltpu.VMEM((count, 2, mate, lc), I16),
+        pltpu.VMEM((count, 3, mate, lc), I16),
         pltpu.VMEM((count, 2, half, 16, wp), BF16),
         pltpu.VMEM((w // 2, w), BF16),
         pltpu.VMEM((sets, w // 2, rt * 16), BF16),
@@ -536,7 +546,7 @@
         dma((sets, 2, 2)), dma((sets, 2)),
         dma((1,)), dma((count, n_row)), dma((count,)),
         dma((1,)), dma((count, hops)),
-        dma((1,)), dma((count,)),
+        dma((2,)), dma((count, 2)),
         dma((1,)), dma((count,)),
         dma((1,)), dma((count,)),
         dma((1,)), dma((count,)),

time: 125 us -> 120 us (0.960)
  Pallas kernels: 121 us -> 117 us
    pallas_call x1, Pallas kernels: 121 us -> 117 us  [body(): pl.pallas_call(functools.partial(kernel, n_row, n_col), out_shape=(jax.Sh...]
where the time goes in v5:
time: 120 us
  Pallas kernels  117 us (98%)
  local copies, waits for them, and re-layouts  3 us (2%)
    pallas_call x1, Pallas kernels, body(): pl.pallas_call(functools.partial(kernel, n_row, n_col), out_shape=(jax.Sh...  117 us
    unnamed x2, local copies, waits for them, and re-layouts  3 us

profile of v5, /device:TPU:24, one launch (start us, length us, event | category | flops | bytes accessed | tf_op | source)
XLA Modules:
  0.0 120.2 jit_solution(10007899648834602169)
XLA Ops:
  0.6 116.6 %selected_inverse.1 = (bf16[3,12,8,512]{3,2,1,0:T(8,128)(2,1)}, f32[3,2,512]{2,1,0:T(2,128)}) custom-call(s32[3,96]{1,0:T(4,128)} %mask_ref.1, bf16[12,3,2,8,16,256]{5,4,3,2,1,0:T(8,128)(2,1)} %bitcast.7, bf16[3,12,8,512]{3,2,1,0:T(8,128)(2,1)} %bitcast.9, f32[3,2,512]{2,1,0:T(2,128)} %dinv_ref.1), custom_call_target="tpu_custom_call" | custom-call | tf_op jit(solution)/shard_map/selected_inverse/pallas_call | solution.py:555
  117.2 1.7 %copy.9 = bf16[3,12,1,8,512]{4,3,2,1,0:T(8,128)(2,1)} copy(bf16[3,12,1,8,512]{4,3,2,1,0:T(8,128)(2,1)} %bitcast.8) | data formatting | bytes 589824
  118.9 1.3 %copy.10 = f32[3,2,512]{2,1,0:T(2,128)} copy(f32[3,2,512]{2,1,0:T(2,128)} %get-tuple-element.11) | data formatting | bytes 24576
